TPU v7x, 32 devices: a whole 2x2x4 slice. The times are simulated.
32 devices in a mesh: node: 4 (over x, core), dev: 8 (over z, y).
Axes of the slice: x: 2, y: 2, z: 4, core: 2. Of those that a mesh axis runs over, the one named last changes fastest.
Arguments:
- tokens: bfloat16 [8192, 7168], P(('node', 'dev')), may hold values from -6 to 6
- grad_out: bfloat16 [8192, 7168], P(('node', 'dev')), may hold values from -1.796875 to 1.796875
- router_gates: bfloat16 [8192, 8], P(('node', 'dev')), may hold values from 0.049804688 to 1
- expert_ids: int32 [8192, 8], P(('node', 'dev')), may hold values from 0 to 255, as said below
- slot_plan: int32 [256, 2], replicated, may hold values from 0 to 8, as said below
- w_gate: bfloat16 [4, 7168, 2048], P(None, 'dev', 'node'), may hold values from -0.0625 to 0.0625
- w_up: bfloat16 [4, 7168, 2048], P(None, 'dev', 'node'), may hold values from -0.0625 to 0.0625
- w_down: bfloat16 [4, 2048, 7168], P(None, 'node', 'dev'), may hold values from -0.125 to 0.125
Outputs:
- grad_tokens: bfloat16 [8192, 7168], P(('node', 'dev'))
- grad_gates: float32 [8192, 8], P(('node', 'dev'))
- grad_w_gate: bfloat16 [4, 7168, 2048], P(None, 'dev', 'node')
- grad_w_up: bfloat16 [4, 7168, 2048], P(None, 'dev', 'node')
- grad_w_down: bfloat16 [4, 2048, 7168], P(None, 'node', 'dev')
Inputs may be any that keep to these rules, and one draw needn't show every extreme that they name: `expert_ids`: each token names 8 different experts. Within one block of 256 tokens (the tokens of one device), at most 4 pairs name any one expert that has slots, and in every draw one expert that has slots is named exactly 2 * 2 times in every block. `slot_plan`: exactly 4 rows hold slots: each such row holds two different slots, and every slot 0 .. 7 stands in exactly one row. Every entry of the other rows equals 8.
All inputs are finite; a program needn't handle non-finite values.
Results may differ from a plain program's by a relative error of at most 0.0059.
Values may be sent and summed in bfloat16 or wider, within the bound.
A program may use at most 128 MiB of HBM per device.

v0:
```python
import jax
import jax.numpy as jnp
from jax import lax
from jax.sharding import PartitionSpec as P

EXPERTS = 256
TOP = 8
CAP = 2


def expert_pass(pieces, slot_gate, slot_up, slot_down):
    x_piece, dy_piece, gate_piece = pieces
    lead_count = x_piece.shape[0]
    slot_count = slot_down.shape[0]
    model_width = x_piece.shape[-1]
    x_rows = x_piece.reshape(-1, model_width)
    dy_split = dy_piece.reshape(-1, slot_count, model_width // slot_count)
    gate_rows = gate_piece.reshape(-1, 1).astype(jnp.float32)
    gate_pre = jnp.dot(x_rows, slot_gate, preferred_element_type=jnp.float32)
    up_pre = jnp.dot(x_rows, slot_up, preferred_element_type=jnp.float32)
    back_proj = jnp.einsum("rsk,shk->rh", dy_split, slot_down, preferred_element_type=jnp.float32)
    sigmoid_gate = jax.nn.sigmoid(gate_pre)
    active = gate_pre * sigmoid_gate
    hidden = active * up_pre
    scaled_back = gate_rows * back_proj
    d_gate = (scaled_back * up_pre * sigmoid_gate * (1.0 + gate_pre * (1.0 - sigmoid_gate))).astype(
        jnp.bfloat16
    )
    d_up = (scaled_back * active).astype(jnp.bfloat16)
    scaled_hidden = (gate_rows * hidden).astype(jnp.bfloat16)
    gate_terms = jnp.sum(back_proj * hidden, axis=-1)
    row_terms = jnp.einsum("rh,dh->rd", d_gate, slot_gate, preferred_element_type=jnp.float32)
    row_terms = row_terms + jnp.einsum(
        "rh,dh->rd", d_up, slot_up, preferred_element_type=jnp.float32
    )
    acc_gate = jnp.einsum("rd,rh->dh", x_rows, d_gate, preferred_element_type=jnp.float32)
    acc_up = jnp.einsum("rd,rh->dh", x_rows, d_up, preferred_element_type=jnp.float32)
    acc_down = jnp.einsum(
        "rsk,rh->shk", dy_split, scaled_hidden, preferred_element_type=jnp.float32
    )
    row_acc = row_terms.reshape(lead_count, slot_count, -1, model_width)
    gate_acc = gate_terms.reshape(lead_count, slot_count, -1)
    return (acc_gate, acc_up, acc_down, row_acc, gate_acc)


def local(tokens, grad_out, router_gates, expert_ids, slot_plan, w_gate, w_up, w_down):
    slot_count = lax.axis_size("dev")
    tok_rows, model_width = tokens.shape
    hidden_width = w_gate.shape[2]
    round_total = w_gate.shape[0]
    pair_total = tok_rows * TOP
    expert_match = expert_ids[:, :, None] == jnp.arange(EXPERTS, dtype=jnp.int32)
    first_slot = jnp.sum(jnp.where(expert_match, slot_plan[:, 0], 0), axis=-1).reshape(pair_total)
    second_slot = jnp.sum(jnp.where(expert_match, slot_plan[:, 1], 0), axis=-1).reshape(pair_total)
    is_live = first_slot < slot_count
    first_hot = (first_slot[:, None] == jnp.arange(slot_count, dtype=jnp.int32)[None, :]).astype(
        jnp.int32
    )
    pair_order = jnp.sum(first_hot * (jnp.cumsum(first_hot, axis=0) - 1), axis=-1)
    pair_slot = jnp.where(pair_order % 2 == 0, first_slot, second_slot)
    target_row = pair_slot * CAP + pair_order // 2
    position_ids = jnp.arange(slot_count * CAP, dtype=jnp.int32)
    chooser = (is_live[None, :] & (target_row[None, :] == position_ids[:, None])).astype(
        jnp.float32
    )
    pick_rows = jnp.sum(chooser.reshape(slot_count * CAP, tok_rows, TOP), axis=-1)
    pick_half = pick_rows.astype(jnp.bfloat16)
    x_send = (
        jnp.dot(pick_half, tokens, preferred_element_type=jnp.float32)
        .astype(jnp.bfloat16)
        .reshape(slot_count, CAP, model_width)
    )
    dy_send = (
        jnp.dot(pick_half, grad_out, preferred_element_type=jnp.float32)
        .astype(jnp.bfloat16)
        .reshape(slot_count, CAP, model_width)
    )
    flat_gates = router_gates.reshape(pair_total).astype(jnp.float32)
    gate_send = (
        jnp.dot(chooser, flat_gates, precision=lax.Precision.HIGHEST)
        .astype(jnp.bfloat16)
        .reshape(slot_count, CAP)
    )
    in_round = (slot_plan[:, 0] < slot_count).astype(jnp.int32)
    expert_rank = jnp.cumsum(in_round) - 1
    holder = jnp.any(slot_plan[:, :, None] == jnp.arange(slot_count, dtype=jnp.int32), axis=1)
    slot_rank = jnp.sum(jnp.where(holder, expert_rank[:, None], 0), axis=0)
    grouping = (slot_rank[None, :] == jnp.arange(round_total, dtype=jnp.int32)[:, None]).astype(
        jnp.bfloat16
    )
    copy_gate = jnp.take(w_gate, slot_rank, axis=0)
    copy_up = jnp.take(w_up, slot_rank, axis=0)
    copy_down = jnp.take(w_down, slot_rank, axis=0)
    slot_gate, slot_up, slot_down = (
        lax.all_to_all(copy_gate, "dev", split_axis=0, concat_axis=0, tiled=True),
        lax.all_to_all(copy_up, "dev", split_axis=0, concat_axis=0, tiled=True),
        lax.all_to_all(copy_down, "dev", split_axis=0, concat_axis=0, tiled=True),
    )
    slot_gate = slot_gate.reshape(model_width, hidden_width)
    slot_up = slot_up.reshape(model_width, hidden_width)
    got_x, got_dy, got_gate = (
        lax.all_to_all(x_send, "dev", split_axis=0, concat_axis=0, tiled=True),
        lax.all_to_all(dy_send, "dev", split_axis=0, concat_axis=0, tiled=True),
        lax.all_to_all(gate_send, "dev", split_axis=0, concat_axis=0, tiled=True),
    )
    totals = expert_pass(
        (
            lax.all_gather(got_x[None], "node", axis=0, tiled=True),
            lax.all_gather(got_dy[None], "node", axis=0, tiled=True),
            lax.all_gather(got_gate[None], "node", axis=0, tiled=True),
        ),
        slot_gate,
        slot_up,
        slot_down,
    )
    acc_gate, acc_up, acc_down, row_acc, gate_acc = totals
    summed_rows, summed_gates = (
        lax.psum_scatter(row_acc, "node", scatter_dimension=0, tiled=True),
        lax.psum_scatter(gate_acc, "node", scatter_dimension=0, tiled=True),
    )
    back_rows, back_gates = (
        lax.all_to_all(summed_rows, "dev", split_axis=1, concat_axis=1, tiled=True),
        lax.all_to_all(summed_gates, "dev", split_axis=1, concat_axis=1, tiled=True),
    )
    grad_tokens = jnp.einsum(
        "qt,qd->td",
        pick_rows,
        back_rows.reshape(slot_count * CAP, model_width),
        precision=lax.Precision.HIGHEST,
    ).astype(jnp.bfloat16)
    grad_gates = jnp.dot(
        back_gates.reshape(slot_count * CAP), chooser, precision=lax.Precision.HIGHEST
    ).reshape(tok_rows, TOP)
    send_gate = acc_gate.astype(jnp.bfloat16).reshape(
        slot_count, model_width // slot_count, hidden_width
    )
    send_up = acc_up.astype(jnp.bfloat16).reshape(
        slot_count, model_width // slot_count, hidden_width
    )
    send_down = acc_down.astype(jnp.bfloat16)
    got_wgate, got_wup, got_wdown = (
        lax.all_to_all(send_gate, "dev", split_axis=0, concat_axis=0, tiled=True),
        lax.all_to_all(send_up, "dev", split_axis=0, concat_axis=0, tiled=True),
        lax.all_to_all(send_down, "dev", split_axis=0, concat_axis=0, tiled=True),
    )
    grad_w_gate = jnp.einsum(
        "js,sdh->jdh", grouping, got_wgate, preferred_element_type=jnp.float32
    ).astype(jnp.bfloat16)
    grad_w_up = jnp.einsum(
        "js,sdh->jdh", grouping, got_wup, preferred_element_type=jnp.float32
    ).astype(jnp.bfloat16)
    grad_w_down = jnp.einsum(
        "js,shk->jhk", grouping, got_wdown, preferred_element_type=jnp.float32
    ).astype(jnp.bfloat16)
    return (grad_tokens, grad_gates, grad_w_gate, grad_w_up, grad_w_down)


def solution(mesh):
    return jax.shard_map(
        local,
        mesh=mesh,
        in_specs=(
            P(("node", "dev"), None),
            P(("node", "dev"), None),
            P(("node", "dev"), None),
            P(("node", "dev"), None),
            P(),
            P(None, "dev", "node"),
            P(None, "dev", "node"),
            P(None, "node", "dev"),
        ),
        out_specs=(
            P(("node", "dev"), None),
            P(("node", "dev"), None),
            P(None, "dev", "node"),
            P(None, "dev", "node"),
            P(None, "node", "dev"),
        ),
        check_vma=False,
    )
```

profile of v0, /device:TPU:0, one launch (start us, length us, event | category | flops | bytes accessed | tf_op | source)
XLA Modules:
  0.0 1153.5 jit_solution(5073613457967397045)
XLA Ops:
  7.2 0.8 fusion.54
  7.9 0.8 copy.89
  8.8 9.2 select_reduce_fusion
  18.2 2.3 reduce-window.15
  21.1 0.8 copy.97
  22.4 0.7 all_to_all.48
  23.0 7.3 all-to-all-start
  30.6 0.7 fusion.37
  31.3 0.7 compare_convert_fusion
  32.1 2.6 convolution_convert_fusion.3
  34.7 0.8 reshape.235
  36.3 6.1 gather_fusion.1
  42.4 6.0 gather_fusion.2
  48.3 6.0 all-to-all-start.3
  54.3 2.6 convolution_convert_fusion.4
  57.0 0.8 reshape.232
  57.8 4.6 all-to-all-done.3
  62.4 3.4 all-to-all-start.1
  65.8 10.6 broadcast_select_fusion.1
  76.4 165.5 %all_to_all.60 = bf16[8,896,512]{2,1,0:T(8,128)(2,1)} all-to-all(bf16[8,896,512]{2,1,0:T(8,128)(2,1)} %get-tuple-element.43), channel_id=1, replica_groups=mesh['node'=4,'dev'=8] {'dev'}, dimensions={0} | all-to-all | bytes 14680064 | tf_op jit(solution)/shard_map/all_to_all | solution.py:96
  241.8 4.8 all-to-all-start.5
  246.7 6.4 gather_fusion
  253.1 6.8 broadcast_select_fusion.2
  260.0 146.3 %all-to-all-done.5 = bf16[8,896,512]{2,1,0:T(8,128)(2,1)} async-done(((bf16[8,896,512]{2,1,0:T(8,128)(2,1)}), bf16[8,896,512]{2,1,0:T(8,128)(2,1)}, u32[]{:S(2)}, u32[]{:S(2)}) %all-to-all-start.5) | async-done | bytes 7340064 | tf_op jit(solution)/shard_map/all_to_all | solution.py:95
  406.2 4.8 all-to-all-start.2
  411.1 5.2 all-gather
  416.4 9.9 all-gather.2
  426.6 9.4 all-gather.1
  436.7 4.5 fusion.55
  441.1 4.5 fusion.56
  445.6 125.1 %all-to-all-done.2 = bf16[8,512,896]{2,1,0:T(8,128)(2,1)} async-done(((bf16[8,512,896]{2,1,0:T(8,128)(2,1)}), bf16[8,512,896]{2,1,0:T(8,128)(2,1)}, u32[]{:S(2)}, u32[]{:S(2)}) %all-to-all-start.2) | async-done | bytes 7340064 | tf_op jit(solution)/shard_map/all_to_all | solution.py:97
  570.7 5.7 multiply_reduce_fusion
  576.4 5.5 fusion.57
  582.0 3.6 convolution_add_fusion
  585.6 3.3 reshape.239
  588.8 3.3 copy.100
  592.1 0.6 dynamic-slice
  592.9 5.6 all-reduce
  598.6 0.7 constant_dynamic-slice_fusion
  599.2 0.7 copy.103
  599.9 4.9 all-to-all-start.7
  604.8 16.4 %reduce-scatter.2.cloned.1.call-done = f32[1,8,2,7168]{3,1,2,0:T(8,128)} async-done(((f32[4,8,2,7168]{3,1,2,0:T(8,128)}), f32[1,8,2,7168]{3,1,2,0:T(8,128)}) %reduce-scatter.2.cloned.1.call-update) | async-done | bytes 458768 | tf_op jit(solution)/shard_map/reduce_scatter | solution.py:118
  621.2 2.1 copy.101
  623.4 5.5 all-to-all-start.6
  628.9 5.1 convolution_convert_fusion.1
  634.0 8.0 all-to-all-done.6
  642.0 5.0 all-to-all-start.8
  647.0 5.1 convolution_convert_fusion
  652.1 154.6 %all-to-all-done.8 = bf16[8,896,512]{2,1,0:T(8,128)(2,1)} async-done(((bf16[8,896,512]{2,1,0:T(8,128)(2,1)}), bf16[8,896,512]{2,1,0:T(8,128)(2,1)}, u32[]{:S(2)}, u32[]{:S(2)}) %all-to-all-start.8) | async-done | bytes 7340064 | tf_op jit(solution)/shard_map/all_to_all | solution.py:142
  806.6 4.8 all-to-all-start.9
  811.5 5.1 convert_bitcast_fusion
  816.6 154.5 %all-to-all-done.9 = bf16[8,896,512]{2,1,0:T(8,128)(2,1)} async-done(((bf16[8,896,512]{2,1,0:T(8,128)(2,1)}), bf16[8,896,512]{2,1,0:T(8,128)(2,1)}, u32[]{:S(2)}, u32[]{:S(2)}) %all-to-all-start.9) | async-done | bytes 7340064 | tf_op jit(solution)/shard_map/all_to_all | solution.py:143
  971.1 4.9 all-to-all-start.10
  976.5 0.7 reduce.11
  977.2 1.0 fusion.24
  978.2 0.9 copy.111
  979.5 7.6 convolution_convert_fusion.2
  987.0 7.9 fusion.6
  994.9 2.6 copy.108
  997.5 7.9 fusion.9
  1005.3 2.6 copy.109
  1007.9 127.9 %all-to-all-done.10 = bf16[8,512,896]{2,1,0:T(8,128)(2,1)} async-done(((bf16[8,512,896]{2,1,0:T(8,128)(2,1)}), bf16[8,512,896]{2,1,0:T(8,128)(2,1)}, u32[]{:S(2)}, u32[]{:S(2)}) %all-to-all-start.10) | async-done | bytes 7340064 | tf_op jit(solution)/shard_map/all_to_all | solution.py:144
  1135.8 8.1 fusion.12
  1143.9 2.3 copy.110
  (51 shorter events, 4.6 us)
Async XLA Ops:
  23.0 25.3 %all-to-all-start = ((bf16[8,1,2]{2,1,0:T(2,128)(2,1)}), bf16[8,1,2]{2,1,0:T(2,128)(2,1)S(1)}, u32[]{:S(2)}, u32[]{:S(2)}) async-start(bf16[8,1,2]{2,1,0:T(2,128)(2,1)} %all_to_all.48), calls=%async_computation | async-start | bytes 8192 | tf_op jit(solution)/shard_map/all_to_all | solution.py:104
  48.3 14.0 %all-to-all-start.3 = ((bf16[8,2,7168]{2,1,0:T(2,128)(2,1)}), bf16[8,2,7168]{2,1,0:T(2,128)(2,1)S(1)}, u32[]{:S(2)}, u32[]{:S(2)}) async-start(bf16[8,2,7168]{2,1,0:T(2,128)(2,1)} %reshape.235), calls=%async_computation.3 | async-start | bytes 458752 | tf_op jit(solution)/shard_map/all_to_all | solution.py:102
  62.4 14.0 %all-to-all-start.1 = ((bf16[8,2,7168]{2,1,0:T(2,128)(2,1)}), bf16[8,2,7168]{2,1,0:T(2,128)(2,1)S(1)}, u32[]{:S(2)}, u32[]{:S(2)}) async-start(bf16[8,2,7168]{2,1,0:T(2,128)(2,1)} %reshape.232), calls=%async_computation.1 | async-start | bytes 458752 | tf_op jit(solution)/shard_map/all_to_all | solution.py:103
  241.8 164.4 %all-to-all-start.5 = ((bf16[8,896,512]{2,1,0:T(8,128)(2,1)}), bf16[8,896,512]{2,1,0:T(8,128)(2,1)}, u32[]{:S(2)}, u32[]{:S(2)}) async-start(bf16[8,896,512]{2,1,0:T(8,128)(2,1)} %get-tuple-element.44), calls=%async_computation.5 | async-start | bytes 14680064 | tf_op jit(solution)/shard_map/all_to_all | solution.py:95
  406.2 164.5 %all-to-all-start.2 = ((bf16[8,512,896]{2,1,0:T(8,128)(2,1)}), bf16[8,512,896]{2,1,0:T(8,128)(2,1)}, u32[]{:S(2)}, u32[]{:S(2)}) async-start(bf16[8,512,896]{2,1,0:T(8,128)(2,1)} %broadcast_select_fusion.2), calls=%async_computation.2 | async-start | bytes 14680064 | tf_op jit(solution)/shard_map/all_to_all | solution.py:97
  411.1 210.2 %reduce-scatter.2.cloned.1.call-start = ((), (), s32[]{:S(2)}) async-start(), calls=%async_computation.12 | async-start | bytes 2293760 | tf_op jit(solution)/shard_map/reduce_scatter | solution.py:118
  570.7 11.3 slice-start
  576.4 5.6 slice-start.1
  585.6 6.6 copy-start
  599.9 23.5 %all-to-all-start.7 = ((f32[1,8,2]{2,0,1:T(1,128)}), f32[1,8,2]{2,0,1:T(1,128)S(1)}, u32[]{:S(2)}, u32[]{:S(2)}) async-start(f32[1,8,2]{2,0,1:T(1,128)} %copy.103), calls=%async_computation.8 | async-start | bytes 8192 | tf_op jit(solution)/shard_map/all_to_all | solution.py:123
  623.4 18.6 %all-to-all-start.6 = ((f32[1,8,2,7168]{3,2,0,1:T(2,128)}), f32[1,8,2,7168]{3,2,0,1:T(2,128)S(1)}, u32[]{:S(2)}, u32[]{:S(2)}) async-start(f32[1,8,2,7168]{3,2,0,1:T(2,128)} %copy.101), calls=%async_computation.7 | async-start | bytes 917504 | tf_op jit(solution)/shard_map/all_to_all | solution.py:122
  642.0 164.7 %all-to-all-start.8 = ((bf16[8,896,512]{2,1,0:T(8,128)(2,1)}), bf16[8,896,512]{2,1,0:T(8,128)(2,1)}, u32[]{:S(2)}, u32[]{:S(2)}) async-start(bf16[8,896,512]{2,1,0:T(8,128)(2,1)} %bitcast.76), calls=%async_computation.9 | async-start | bytes 14680064 | tf_op jit(solution)/shard_map/all_to_all | solution.py:142
  806.6 164.4 %all-to-all-start.9 = ((bf16[8,896,512]{2,1,0:T(8,128)(2,1)}), bf16[8,896,512]{2,1,0:T(8,128)(2,1)}, u32[]{:S(2)}, u32[]{:S(2)}) async-start(bf16[8,896,512]{2,1,0:T(8,128)(2,1)} %bitcast.75), calls=%async_computation.10 | async-start | bytes 14680064 | tf_op jit(solution)/shard_map/all_to_all | solution.py:143
  971.1 164.7 %all-to-all-start.10 = ((bf16[8,512,896]{2,1,0:T(8,128)(2,1)}), bf16[8,512,896]{2,1,0:T(8,128)(2,1)}, u32[]{:S(2)}, u32[]{:S(2)}) async-start(bf16[8,512,896]{2,1,0:T(8,128)(2,1)} %convert_bitcast_fusion), calls=%async_computation.11 | async-start | bytes 14680064 | tf_op jit(solution)/shard_map/all_to_all | solution.py:144
Sparse Core Ops, SparseCore 0:
  592.3 28.9 reduce-scatter.1
where the time goes:
time: 1160 us; the launch traced here: 1150 us
  waiting for transfers between devices  737 us (64%)
  blocking collectives  196 us (17%)
  matrix products  76.8 us (7%)
  starting transfers between devices  51.5 us (4%)
  local copies, waits for them, and re-layouts  45.4 us (4%)
  other arithmetic  32 us (3%)
  between operations  14.8 us (1%)
    all_to_all x1, blocking collectives, local(): lax.all_to_all(copy_up, 'dev', split_axis=0, concat_axis=0, tiled=True)  165 us
    all_to_all x1, waiting for transfers between devices, local(): lax.all_to_all(send_gate, 'dev', split_axis=0, concat_axis=0, tiled=True)  155 us
    all_to_all x1, waiting for transfers between devices, local(): lax.all_to_all(send_up, 'dev', split_axis=0, concat_axis=0, tiled=True)  154 us
    all_to_all x1, waiting for transfers between devices, local(): lax.all_to_all(copy_gate, 'dev', split_axis=0, concat_axis=0, tiled=True)  146 us
    all_to_all x1, waiting for transfers between devices, local(): lax.all_to_all(send_down, 'dev', split_axis=0, concat_axis=0, tiled=True)  128 us
    all_to_all x1, waiting for transfers between devices, local(): lax.all_to_all(copy_down, 'dev', split_axis=0, concat_axis=0, tiled=True)  125 us
  transfers between devices with their start and end apart: 11, of which 8 were waited for; matrix products, arithmetic and copies ran while one was open for 9% of the time, Pallas kernels for 0%

commit v1 on v0

v1 whole, which is shorter than its diff:
```python
import jax
import jax.numpy as jnp
from jax import lax
from jax.sharding import PartitionSpec as P

REPS = 2
CAP = 2
PER = REPS * CAP
F32 = jnp.float32
BF16 = jnp.bfloat16


def choose(expert_ids, router_gates, slot_plan, slots, experts):
    tok = expert_ids.shape[0]
    total = slot_plan.shape[0]
    live = slot_plan[:, 0] < slots
    ids = jnp.arange(total, dtype=jnp.int32)
    rank = jnp.sum(jnp.where((ids[None, :] < ids[:, None]) & live[None, :], 1, 0), axis=1)
    hot = jnp.sum(
        jnp.where(live[None, :] & (rank[None, :] == jnp.arange(experts)[:, None]), ids[None, :], 0),
        axis=1,
    )
    match = expert_ids[None, :, :] == hot[:, None, None]
    named = jnp.any(match, axis=2)
    gate = jnp.sum(jnp.where(match, router_gates.astype(F32)[None], 0.0), axis=2)
    t = jnp.arange(tok)
    before = (t[:, None] < t[None, :]).astype(BF16)
    order = jnp.dot(named.astype(BF16), before, preferred_element_type=F32)
    pick = named[:, None, :] & (order[:, None, :] == jnp.arange(PER, dtype=F32)[None, :, None])
    row_gate = jnp.sum(jnp.where(pick, gate[:, None, :], 0.0), axis=2)
    return pick.reshape(experts * PER, tok).astype(BF16), row_gate.reshape(-1), match


def local(tokens, grad_out, router_gates, expert_ids, slot_plan, w_gate, w_up, w_down):
    nd = lax.axis_size("dev")
    nn = lax.axis_size("node")
    tok, width = tokens.shape
    experts, cols, hid = w_gate.shape
    rows = experts * PER
    pick, row_gate, match = choose(expert_ids, router_gates, slot_plan, nd, experts)
    x_rows = jnp.dot(pick, tokens, preferred_element_type=F32).astype(BF16)
    dy_rows = jnp.dot(pick, grad_out, preferred_element_type=F32).astype(BF16)
    x_rows = x_rows.reshape(rows, nd, cols).transpose(1, 0, 2)
    dy_rows = dy_rows.reshape(rows, nd, cols).transpose(1, 0, 2)
    gate_line = jnp.zeros((1, cols), BF16).at[0, :rows].set(row_gate.astype(BF16))
    gate_line = jnp.broadcast_to(gate_line[None], (nd, 1, cols))
    sent = jnp.concatenate([x_rows, dy_rows, gate_line], axis=1)
    got = lax.all_to_all(sent, "dev", split_axis=0, concat_axis=0, tiled=True)
    got = lax.all_gather(got, "node", axis=0, tiled=False)
    per_expert = nn * nd * PER
    xs = got[:, :, :rows].reshape(nn, nd, experts, PER, cols).transpose(2, 0, 1, 3, 4)
    xs = xs.reshape(experts, per_expert, cols)
    dys = got[:, :, rows : 2 * rows].reshape(nn, nd, experts, PER, cols).transpose(2, 0, 1, 3, 4)
    dys = dys.reshape(experts, per_expert, cols)
    gates = got[:, :, 2 * rows, :rows].reshape(nn, nd, experts, PER).transpose(2, 0, 1, 3)
    part = experts * per_expert // nd
    gates = gates.reshape(nd, part)
    me = lax.axis_index("dev")
    node = lax.axis_index("node")
    my_gate = jnp.sum(
        jnp.where(jnp.arange(nd)[:, None] == me, gates.astype(F32), 0.0), axis=0
    )[:, None]

    def widen(a, b, spec):
        r = jnp.einsum(spec, a, b, preferred_element_type=F32).astype(BF16)
        return r.reshape(nd, part, hid)

    pre = jnp.stack(
        [
            widen(xs, w_gate, "jrd,jdh->jrh"),
            widen(xs, w_up, "jrd,jdh->jrh"),
            widen(dys, w_down, "jrd,jhd->jrh"),
        ],
        axis=1,
    )
    pre = lax.all_to_all(pre, "dev", split_axis=0, concat_axis=0, tiled=True)
    sums = jnp.sum(pre.astype(F32), axis=0)
    gate_pre, up_pre, back = sums[0], sums[1], sums[2]
    sig = jax.nn.sigmoid(gate_pre)
    act = gate_pre * sig
    hidden = act * up_pre
    scaled = my_gate * back
    d_gate = (scaled * up_pre * sig * (1.0 + gate_pre * (1.0 - sig))).astype(BF16)
    d_up = (scaled * act).astype(BF16)
    s_hid = (my_gate * hidden).astype(BF16)
    gate_terms = jnp.sum(back * hidden, axis=-1)
    full = lax.all_gather(jnp.stack([d_gate, d_up, s_hid]), "dev", axis=1, tiled=False)
    full = full.reshape(3, experts, per_expert, hid)
    spread = jnp.where(jnp.arange(nd)[:, None] == me, gate_terms[None, :], 0.0)
    spread = lax.psum(spread.reshape(experts, nn, nd, PER), ("node", "dev"))
    dg, du, sh = full[0], full[1], full[2]
    row_grad = jnp.einsum("jrh,jdh->jrd", dg, w_gate, preferred_element_type=F32)
    row_grad = row_grad + jnp.einsum("jrh,jdh->jrd", du, w_up, preferred_element_type=F32)
    row_grad = row_grad.reshape(experts, nn, nd, PER, cols).transpose(1, 2, 0, 3, 4)
    row_grad = lax.psum_scatter(row_grad, "node", scatter_dimension=0, tiled=False)
    back_rows = lax.all_to_all(row_grad, "dev", split_axis=0, concat_axis=0, tiled=True)
    back_rows = back_rows.reshape(nd, rows, cols).transpose(1, 0, 2).reshape(rows, width)
    high = back_rows.astype(BF16)
    low = (back_rows - high.astype(F32)).astype(BF16)
    grad_tokens = jnp.einsum(
        "qt,qd->td",
        jnp.concatenate([pick, pick], axis=0),
        jnp.concatenate([high, low], axis=0),
        preferred_element_type=F32,
    ).astype(BF16)
    mine = lax.dynamic_slice(spread, (0, node, me, 0), (experts, 1, 1, PER)).reshape(experts, PER, 1)
    pair_val = jnp.sum(jnp.where(pick.reshape(experts, PER, tok) > 0, mine, 0.0), axis=1)
    grad_gates = jnp.sum(jnp.where(match, pair_val[:, :, None], 0.0), axis=0)
    grad_w_gate = jnp.einsum("jrd,jrh->jdh", xs, dg, preferred_element_type=F32).astype(BF16)
    grad_w_up = jnp.einsum("jrd,jrh->jdh", xs, du, preferred_element_type=F32).astype(BF16)
    grad_w_down = jnp.einsum("jrh,jrd->jhd", sh, dys, preferred_element_type=F32).astype(BF16)
    return (grad_tokens, grad_gates, grad_w_gate, grad_w_up, grad_w_down)


def solution(mesh):
    return jax.shard_map(
        local,
        mesh=mesh,
        in_specs=(
            P(("node", "dev"), None),
            P(("node", "dev"), None),
            P(("node", "dev"), None),
            P(("node", "dev"), None),
            P(),
            P(None, "dev", "node"),
            P(None, "dev", "node"),
            P(None, "node", "dev"),
        ),
        out_specs=(
            P(("node", "dev"), None),
            P(("node", "dev"), None),
            P(None, "dev", "node"),
            P(None, "dev", "node"),
            P(None, "node", "dev"),
        ),
        check_vma=False,
    )
```

time: 1160 us -> 243 us (0.21)
  waiting for transfers between devices: 737 us -> 102 us
  blocking collectives: 196 us -> 63.3 us
  matrix products: 76.8 us -> 26.4 us
  starting transfers between devices: 51.5 us -> 10.3 us
  local copies, waits for them, and re-layouts: 45.4 us -> 17.4 us
  other arithmetic: 32 us -> 8.92 us
    all_to_all x10 -> x2, waiting for transfers between devices: 721 us -> 39.6 us  [the longest x1 36.2 us: local(): pre = lax.all_to_all(pre, 'dev', split_axis=0, concat_axis=0, tiled=True)]
    all_to_all x1, blocking collectives: 165 us -> 23.4 us  [local(): got = lax.all_to_all(sent, 'dev', split_axis=0, concat_axis=0, tiled=True)]
    all_gather x0 -> x2, waiting for transfers between devices: none -> 62.3 us  [the longest x1 42.4 us: local(): lax.all_gather(jnp.stack([d_gate, d_up, s_hid]), 'dev', axis=1, tiled=False)]
    dot_general x16 -> x12, matrix products: 76.8 us -> 26.4 us  [the longest x3 4.95 us: widen(): r = jnp.einsum(spec, a, b, preferred_element_type=F32).astype(BF16)]
    all_to_all x10 -> x2, starting transfers between devices: 51.5 us -> 10.2 us  [the longest x1 5.52 us: local(): pre = lax.all_to_all(pre, 'dev', split_axis=0, concat_axis=0, tiled=True)]
    psum x0 -> x1, blocking collectives: none -> 39.9 us  [local(): spread = lax.psum(spread.reshape(experts, nn, nd, PER), ('node', 'dev'))]
    all_gather x3 -> x0, blocking collectives: 24.5 us -> none  [the longest x1 9.85 us: local(): lax.all_gather(got_x[None], 'node', axis=0, tiled=True)]
    gather x3 -> x0, local copies, waits for them, and re-layouts: 18.5 us -> none  [the longest x1 6.4 us: local(): copy_down = jnp.take(w_down, slot_rank, axis=0)]
  transfers between devices with their start and end apart: 11 -> 5, of which waited for: 8 -> 4; matrix products, arithmetic and copies ran while one was open for 9% -> 5% of each run, Pallas kernels for 0% -> 0%
where the time goes in v1:
time: 243 us; the launch traced here: 242 us
  waiting for transfers between devices  102 us (42%)
  blocking collectives  63.3 us (26%)
  matrix products  26.4 us (11%)
  local copies, waits for them, and re-layouts  17.4 us (7%)
  between operations  14 us (6%)
  starting transfers between devices  10.3 us (4%)
  other arithmetic  8.92 us (4%)
    all_gather x1, waiting for transfers between devices, local(): lax.all_gather(jnp.stack([d_gate, d_up, s_hid]), 'dev', axis=1, tiled=False)  42.4 us
    psum x1, blocking collectives, local(): spread = lax.psum(spread.reshape(experts, nn, nd, PER), ('node', 'dev'))  39.9 us
    all_to_all x1, waiting for transfers between devices, local(): pre = lax.all_to_all(pre, 'dev', split_axis=0, concat_axis=0, tiled=True)  36.2 us
    all_to_all x1, blocking collectives, local(): got = lax.all_to_all(sent, 'dev', split_axis=0, concat_axis=0, tiled=True)  23.4 us
    all_gather x1, waiting for transfers between devices, local(): got = lax.all_gather(got, 'node', axis=0, tiled=False)  19.9 us
    reshape x2, local copies, waits for them, and re-layouts, local(): row_grad.reshape(experts, nn, nd, PER, cols).transpose(1, 2, 0, 3, 4)  5.69 us
    all_to_all x1, starting transfers between devices, local(): pre = lax.all_to_all(pre, 'dev', split_axis=0, concat_axis=0, tiled=True)  5.52 us
    dot_general x3, matrix products, widen(): r = jnp.einsum(spec, a, b, preferred_element_type=F32).astype(BF16)  4.95 us
  transfers between devices with their start and end apart: 5, of which 4 were waited for; matrix products, arithmetic and copies ran while one was open for 5% of the time, Pallas kernels for 0%

profile of v1, /device:TPU:0, one launch (start us, length us, event | category | flops | bytes accessed | tf_op | source)
XLA Modules:
  0.0 242.2 jit_solution(8520463488732096171)
XLA Ops:
  7.2 0.6 compare_reduce_fusion.2
  7.9 0.7 compare_reduce_fusion.1
  8.6 0.1 select_reduce_fusion
  8.7 0.1 select_reduce_fusion.4
  8.8 0.1 eq.78
  8.9 0.8 compare_reduce_fusion
  9.7 0.1 fusion.4
  9.9 0.7 convert_element_type.78
  10.5 0.8 fusion.11
  11.3 0.1 select_reduce_fusion.2
  11.4 0.6 convert_select_fusion
  12.1 0.1 broadcast_in_dim.150
  12.2 0.1 compare_and_fusion
  12.3 2.8 %convolution_convert_fusion.1 = bf16[16,7168]{1,0:T(8,128)(2,1)S(1)} fusion(pred[16,256]{1,0:T(8,128)(4,1)S(1)} %compare_and_fusion, bf16[256,7168]{1,0:T(8,128)(2,1)} %param.11), kind=kOutput, calls=%fused_computation.1 | convolution fusion | flops 58834944 | bytes 3903488 | tf_op jit(solution)/shard_map/dot_general | solution.py:42
  15.0 0.3 copy-done.3
  15.3 0.6 convolution_convert_fusion.2
  16.1 23.4 %all_to_all.15 = bf16[8,33,896]{2,1,0:T(8,128)(2,1)S(1)} all-to-all(bf16[8,33,896]{2,1,0:T(8,128)(2,1)S(1)} %pad_maximum_fusion.1), channel_id=1, replica_groups=mesh['node'=4,'dev'=8] {'dev'}, dimensions={0} | all-to-all | bytes 946176 | tf_op jit(solution)/shard_map/all_to_all | solution.py:48
  39.4 0.8 copy.91
  40.3 19.9 %all-gather.5.cloned.1.call-done = bf16[32,33,896]{2,0,1:T(8,128)(2,1)} async-done(((bf16[8,33,896]{2,0,1:T(8,128)(2,1)}), bf16[32,33,896]{2,0,1:T(8,128)(2,1)}) %all-gather.5.cloned.1.call-update) | async-done | bytes 1892368 | tf_op jit(solution)/shard_map/all_gather | solution.py:49
  60.2 1.6 fusion.21
  61.8 0.5 copy.95
  62.3 0.2 reshape.150
  62.5 0.5 copy.97
  63.0 0.2 reshape.152
  63.2 2.9 %convolution_convert_fusion.7 = bf16[4,128,512]{2,1,0:T(8,128)(2,1)S(1)} fusion(bf16[4,128,896]{2,1,0:T(8,128)(2,1)S(1)} %reshape.150, bf16[4,896,512]{2,1,0:T(8,128)(2,1)} %param.16), kind=kOutput, calls=%fused_computation.11 | convolution fusion | flops 470024192 | bytes 5111808 | tf_op jit(solution)/shard_map/jrd,jdh->jrh/dot_general | solution.py:65
  66.1 0.2 copy-done
  66.3 0.7 convolution_convert_fusion.8
  67.1 1.3 copy-done.2
  68.4 1.3 convolution_convert_fusion.6
  69.7 1.3 pad_maximum_fusion
  71.0 5.5 %all-to-all-start.1 = ((bf16[8,3,64,512]{3,2,1,0:T(8,128)(2,1)}), bf16[8,3,64,512]{3,2,1,0:T(8,128)(2,1)S(1)}, u32[]{:S(2)}, u32[]{:S(2)}) async-start(bf16[8,3,64,512]{3,2,1,0:T(8,128)(2,1)} %pad_maximum_fusion), calls=%async_computation.1 | async-start | bytes 3145728 | tf_op jit(solution)/shard_map/all_to_all | solution.py:76
  76.6 0.7 slice_convert_fusion
  77.3 0.1 copy.92
  77.4 0.2 copy.93
  77.5 0.1 reshape.156
  77.6 0.1 select_reduce_fusion.3
  77.7 36.2 %all-to-all-done.1 = bf16[8,3,64,512]{3,2,1,0:T(8,128)(2,1)S(1)} async-done(((bf16[8,3,64,512]{3,2,1,0:T(8,128)(2,1)}), bf16[8,3,64,512]{3,2,1,0:T(8,128)(2,1)S(1)}, u32[]{:S(2)}, u32[]{:S(2)}) %all-to-all-start.1) | async-done | bytes 1572896 | tf_op jit(solution)/shard_map/all_to_all | solution.py:76
  113.9 0.2 convert_reduce_fusion
  114.1 0.7 copy-done.4
  114.9 0.1 multiply_convert_fusion.2
  115.0 0.7 pad_maximum_fusion.2
  115.8 42.4 %all-gather.7.cloned.1.call-done = bf16[3,512,512]{2,1,0:T(8,128)(2,1)} async-done(((bf16[3,64,512]{2,1,0:T(8,128)(2,1)}), bf16[3,512,512]{2,1,0:T(8,128)(2,1)}) %all-gather.7.cloned.1.call-update) | async-done | bytes 1572880 | tf_op jit(solution)/shard_map/all_gather | solution.py:87
  158.2 2.3 fusion.22
  160.4 3.4 %fusion.23 = f32[4,128,896]{2,1,0:T(8,128)S(1)} fusion(bf16[4,128,512]{2,1,0:T(8,128)(2,1)S(1)} %bitcast.91, bf16[4,896,512]{2,1,0:T(8,128)(2,1)} %param.15), kind=kOutput, calls=%fused_computation.70 | convolution fusion | flops 469762048 | bytes 6029312 | tf_op jit(solution)/shard_map/jrh,jdh->jrd/dot_general | solution.py:92
  163.9 2.5 %convolution_add_fusion = f32[4,128,896]{2,1,0:T(8,128)} fusion(f32[4,128,896]{2,1,0:T(8,128)S(1)} %fusion.23, bf16[4,128,512]{2,1,0:T(8,128)(2,1)S(1)} %bitcast.93, bf16[4,896,512]{2,1,0:T(8,128)(2,1)S(1)} %copy-done.1), kind=kOutput, calls=%fused_computation.9 | convolution fusion | flops 470220800 | bytes 7864320 | tf_op jit(solution)/shard_map/jrh,jdh->jrd/dot_general | solution.py:93
  166.4 2.8 %reshape.153 = f32[4,4,8,4,896]{4,3,2,1,0:T(4,128)} reshape(f32[4,128,896]{2,1,0:T(8,128)} %convolution_add_fusion) | data formatting | bytes 3670016 | tf_op jit(solution)/shard_map/reshape | solution.py:94
  169.2 2.9 %copy.120 = f32[4,4,8,4,896]{4,2,3,0,1:T(8,128)} copy(f32[4,4,8,4,896]{4,3,2,1,0:T(4,128)} %reshape.153) | data formatting | bytes 3670016 | tf_op jit(solution)/shard_map/reshape | solution.py:94
  172.2 0.2 fusion.6
  172.4 0.1 broadcast_in_dim.156
  172.4 0.1 copy.104
  172.5 0.1 copy.105
  172.6 0.1 broadcast_select_fusion
  172.7 39.9 %psum.7 = f32[4,4,8,4]{3,0,2,1:T(4,128)S(1)} all-reduce(f32[4,4,8,4]{3,0,2,1:T(4,128)S(1)} %broadcast_select_fusion), channel_id=1, replica_groups=mesh['node'=4,'dev'=8] {'node','dev'}, use_global_device_ids=true, to_apply=%region_10.11 | all-reduce | flops 512 | bytes 4096 | tf_op jit(solution)/shard_map/psum | solution.py:90
  212.7 0.1 select_reduce_fusion.1
  212.8 0.7 fusion.12
  213.4 1.9 copy.102
  215.4 4.7 %all-to-all-start.2 = ((f32[8,4,4,896]{3,2,1,0:T(4,128)}), f32[8,4,4,896]{3,2,1,0:T(4,128)S(1)}, u32[]{:S(2)}, u32[]{:S(2)}) async-start(f32[8,4,4,896]{3,2,1,0:T(4,128)} %copy.102), calls=%async_computation.3 | async-start | bytes 917504 | tf_op jit(solution)/shard_map/all_to_all | solution.py:96
  220.1 3.0 %convolution_convert_fusion.4 = bf16[4,896,512]{2,1,0:T(8,128)(2,1)} fusion(bf16[4,128,896]{2,1,0:T(8,128)(2,1)S(1)} %reshape.150, bf16[4,128,512]{2,1,0:T(8,128)(2,1)S(1)} %bitcast.94), kind=kOutput, calls=%fused_computation.5 | convolution fusion | flops 471597056 | bytes 5111808 | tf_op jit(solution)/shard_map/jrd,jrh->jdh/dot_general | solution.py:110
  223.1 3.0 %convolution_convert_fusion.5 = bf16[4,896,512]{2,1,0:T(8,128)(2,1)} fusion(bf16[4,128,896]{2,1,0:T(8,128)(2,1)S(1)} %reshape.150, bf16[4,128,512]{2,1,0:T(8,128)(2,1)S(1)} %bitcast.92), kind=kOutput, calls=%fused_computation.6 | convolution fusion | flops 471597056 | bytes 5111808 | tf_op jit(solution)/shard_map/jrd,jrh->jdh/dot_general | solution.py:109
  226.1 3.0 %convolution_convert_fusion.3 = bf16[4,512,896]{2,1,0:T(8,128)(2,1)} fusion(bf16[4,128,512]{2,1,0:T(8,128)(2,1)S(1)} %bitcast.99, bf16[4,128,896]{2,1,0:T(8,128)(2,1)S(1)} %reshape.152), kind=kOutput, calls=%fused_computation.4 | convolution fusion | flops 471597056 | bytes 5111808 | tf_op jit(solution)/shard_map/jrh,jrd->jhd/dot_general | solution.py:111
  229.1 3.4 %all-to-all-done.2 = f32[8,4,4,896]{3,2,1,0:T(4,128)S(1)} async-done(((f32[8,4,4,896]{3,2,1,0:T(4,128)}), f32[8,4,4,896]{3,2,1,0:T(4,128)S(1)}, u32[]{:S(2)}, u32[]{:S(2)}) %all-to-all-start.2) | async-done | bytes 458784 | tf_op jit(solution)/shard_map/all_to_all | solution.py:96
  232.4 0.1 copy.103
  232.6 0.1 copy.116
  232.7 3.0 %convolution_convert_fusion = bf16[256,7168]{1,0:T(8,128)(2,1)} fusion(bf16[16,7168]{1,0:T(8,128)(2,1)S(1)} %get-tuple-element.17, bf16[16,7168]{1,0:T(8,128)(2,1)S(1)} %get-tuple-element.18, pred[16,256]{1,0:T(8,128)(4,1)S(1)} %compare_and_fusion), kind=kOutput, calls=%fused_computation | convolution fusion | flops 120201216 | bytes 4132864 | tf_op jit(solution)/shard_map/qt,qd->td/dot_general | solution.py:100
  (35 shorter events, 0.5 us)
Async XLA Ops:
  7.2 53.0 %all-gather.5.cloned.1.call-start = ((), (), s32[]{:S(2)}) async-start(), calls=%async_computation.5 | async-start | bytes 2365440 | tf_op jit(solution)/shard_map/all_gather | solution.py:49
  12.2 3.1 %copy-start.3 = (bf16[256,7168]{1,0:T(8,128)(2,1)S(1)}, bf16[256,7168]{1,0:T(8,128)(2,1)}, u32[]{:S(2)}) copy-start(bf16[256,7168]{1,0:T(8,128)(2,1)} %param.10) | copy-start | bytes 11010052
  63.2 3.1 %copy-start = (bf16[4,896,512]{2,1,0:T(8,128)(2,1)S(1)}, bf16[4,896,512]{2,1,0:T(8,128)(2,1)}, u32[]{:S(2)}) copy-start(bf16[4,896,512]{2,1,0:T(8,128)(2,1)} %param.15) | copy-start | bytes 11010052
  66.3 2.0 copy-start.2
  71.0 42.9 %all-to-all-start.1 = ((bf16[8,3,64,512]{3,2,1,0:T(8,128)(2,1)}), bf16[8,3,64,512]{3,2,1,0:T(8,128)(2,1)S(1)}, u32[]{:S(2)}, u32[]{:S(2)}) async-start(bf16[8,3,64,512]{3,2,1,0:T(8,128)(2,1)} %pad_maximum_fusion), calls=%async_computation.1 | async-start | bytes 3145728 | tf_op jit(solution)/shard_map/all_to_all | solution.py:76
  76.5 81.7 %all-gather.7.cloned.1.call-start = ((), (), s32[]{:S(2)}) async-start(), calls=%async_computation.6 | async-start | bytes 1769472 | tf_op jit(solution)/shard_map/all_gather | solution.py:87
  114.1 0.7 copy-start.4
  115.7 97.7 %reduce-scatter.2.cloned.1.call-start = ((), (), s32[]{:S(2)}) async-start(), calls=%async_computation.4 | async-start | bytes 2293760 | tf_op jit(solution)/shard_map/reduce_scatter | solution.py:95
  160.4 3.5 %copy-start.1 = (bf16[4,896,512]{2,1,0:T(8,128)(2,1)S(1)}, bf16[4,896,512]{2,1,0:T(8,128)(2,1)}, u32[]{:S(2)}) copy-start(bf16[4,896,512]{2,1,0:T(8,128)(2,1)} %param.16) | copy-start | bytes 11010052
  169.2 3.0 %copy-start.5 = (f32[3,64,512]{2,1,0:T(8,128)S(1)}, f32[3,64,512]{2,1,0:T(8,128)}, u32[]{:S(2)}) copy-start(f32[3,64,512]{2,1,0:T(8,128)} %copy-done.4) | copy-start | bytes 1179652
  169.2 43.6 %copy-start.7 = (s32[256,8]{0,1:T(8,128)S(1)}, s32[256,8]{0,1:T(8,128)}, u32[]{:S(2)}) copy-start(s32[256,8]{0,1:T(8,128)} %param.13) | copy-start | bytes 24580
  215.4 17.1 %all-to-all-start.2 = ((f32[8,4,4,896]{3,2,1,0:T(4,128)}), f32[8,4,4,896]{3,2,1,0:T(4,128)S(1)}, u32[]{:S(2)}, u32[]{:S(2)}) async-start(f32[8,4,4,896]{3,2,1,0:T(4,128)} %copy.102), calls=%async_computation.3 | async-start | bytes 917504 | tf_op jit(solution)/shard_map/all_to_all | solution.py:96
  223.1 3.0 %copy-start.6 = (bf16[1,512,512]{2,1,0:T(8,128)(2,1)S(1)}, bf16[1,512,512]{2,1,0:T(8,128)(2,1)}, u32[]{:S(2)}) copy-start(bf16[1,512,512]{2,1,0:T(8,128)(2,1)} %get-tuple-element.21) | copy-start | bytes 1572868
Sparse Core Ops, SparseCore 0:
  40.4 19.7 all-gather.4
  115.8 42.3 all-gather.6
  172.3 28.6 reduce-scatter.1

commit v2 on v1

--- a/solution.py
+++ b/solution.py
@@ -1,6 +1,10 @@
+import functools
+
 import jax
 import jax.numpy as jnp
 from jax import lax
+from jax.experimental import pallas as pl
+from jax.experimental.pallas import tpu as pltpu
 from jax.sharding import PartitionSpec as P
 
 REPS = 2
@@ -8,6 +12,130 @@
 PER = REPS * CAP
 F32 = jnp.float32
 BF16 = jnp.bfloat16
+
+
+NZ = 4
+MESH = pl.DeviceIdType.MESH
+
+
+def middle_kernel(
+    nd, hid, pre, gate, full, from_y, stage, from_z, ys, yr, zs, zr, bs, br, fs, fr
+):
+    ny = nd // NZ
+    me = lax.axis_index("dev")
+    z = me // ny
+    y = me % ny
+    barrier = pltpu.get_barrier_semaphore()
+    for i in range(1, ny):
+        peer = z * ny + (y + i) % ny
+        pl.semaphore_signal(barrier, inc=1, device_id={"dev": peer}, device_id_type=MESH)
+    for k in range(1, NZ):
+        peer = ((z + k) % NZ) * ny + y
+        pl.semaphore_signal(barrier, inc=1, device_id={"dev": peer}, device_id_type=MESH)
+    pl.semaphore_wait(barrier, ny - 1 + NZ - 1)
+
+    def remote(src, dst, send, recv, peer):
+        return pltpu.make_async_remote_copy(
+            src_ref=src,
+            dst_ref=dst,
+            send_sem=send,
+            recv_sem=recv,
+            device_id={"dev": peer},
+            device_id_type=MESH,
+        )
+
+    order = [k % NZ for k in range(1, NZ + 1)]
+    first = {}
+    for k in order:
+        zk = (z + k) % NZ
+        for i in range(1, ny):
+            yi = (y + i) % ny
+            c = remote(
+                pre.at[zk * ny + yi], from_y.at[i, k], ys.at[i, k], yr.at[i, k], z * ny + yi
+            )
+            c.start()
+            first[i, k] = c
+    second = {}
+    total = None
+    for k in order:
+        zk = (z + k) % NZ
+        acc = pre[zk * ny + y].astype(F32)
+        for i in range(1, ny):
+            first[i, k].wait_recv()
+            acc = acc + from_y[i, k].astype(F32)
+        if k:
+            stage[k] = acc.astype(BF16)
+            c = remote(stage.at[k], from_z.at[k], zs.at[k], zr.at[k], zk * ny + y)
+            c.start()
+            second[k] = c
+        else:
+            total = acc
+    for k in range(1, NZ):
+        second[k].wait_recv()
+        total = total + from_z[k].astype(F32)
+    g, u, b = total[:, :hid], total[:, hid : 2 * hid], total[:, 2 * hid :]
+    rg = gate[:, 0:1]
+    sig = jax.nn.sigmoid(g)
+    act = g * sig
+    hidden = act * u
+    scaled = rg * b
+    terms = jnp.sum(b * hidden, axis=1, keepdims=True)
+    t1 = terms.astype(BF16).astype(F32)
+    t2 = (terms - t1).astype(BF16).astype(F32)
+    t3 = terms - t1 - t2
+    lane = lax.broadcasted_iota(jnp.int32, (g.shape[0], 128), 1)
+    tail = jnp.where(lane == 0, t1, jnp.where(lane == 1, t2, jnp.where(lane == 2, t3, 0.0)))
+    full[me, :, :hid] = (scaled * u * sig * (1.0 + g * (1.0 - sig))).astype(BF16)
+    full[me, :, hid : 2 * hid] = (scaled * act).astype(BF16)
+    full[me, :, 2 * hid : 3 * hid] = (rg * hidden).astype(BF16)
+    full[me, :, 3 * hid :] = tail.astype(BF16)
+    third = {}
+    fourth = {}
+    for k in range(1, NZ):
+        c = remote(full.at[me], full.at[me], bs.at[k], br.at[k], ((z + k) % NZ) * ny + y)
+        c.start()
+        third[k] = c
+    for k in range(NZ):
+        src = ((z + NZ - k) % NZ) * ny + y
+        if k:
+            third[k].wait_recv()
+        for i in range(1, ny):
+            c = remote(full.at[src], full.at[src], fs.at[i, k], fr.at[i, k], z * ny + (y + i) % ny)
+            c.start()
+            fourth[i, k] = c
+    for c in fourth.values():
+        c.wait_recv()
+    for group in (first, second, third, fourth):
+        for c in group.values():
+            c.wait_send()
+
+
+def middle(pre, gate, hid):
+    nd, part, wide = pre.shape
+    ny = nd // NZ
+    dma = pltpu.SemaphoreType.DMA
+    return pl.pallas_call(
+        functools.partial(middle_kernel, nd, hid),
+        out_shape=jax.ShapeDtypeStruct((nd, part, wide + 128), BF16),
+        in_specs=[pl.BlockSpec(memory_space=pltpu.VMEM)] * 2,
+        out_specs=pl.BlockSpec(memory_space=pltpu.VMEM),
+        scratch_shapes=[
+            pltpu.VMEM((ny, NZ, part, wide), BF16),
+            pltpu.VMEM((NZ, part, wide), BF16),
+            pltpu.VMEM((NZ, part, wide), BF16),
+            dma((ny, NZ)),
+            dma((ny, NZ)),
+            dma((NZ,)),
+            dma((NZ,)),
+            dma((NZ,)),
+            dma((NZ,)),
+            dma((ny, NZ)),
+            dma((ny, NZ)),
+        ],
+        compiler_params=pltpu.CompilerParams(
+            collective_id=0, has_side_effects=True, vmem_limit_bytes=48 * 1024 * 1024
+        ),
+    )(pre, gate)
 
 
 def choose(expert_ids, router_gates, slot_plan, slots, experts):
@@ -42,21 +170,21 @@
     dy_rows = jnp.dot(pick, grad_out, preferred_element_type=F32).astype(BF16)
     x_rows = x_rows.reshape(rows, nd, cols).transpose(1, 0, 2)
     dy_rows = dy_rows.reshape(rows, nd, cols).transpose(1, 0, 2)
-    gate_line = jnp.zeros((1, cols), BF16).at[0, :rows].set(row_gate.astype(BF16))
-    gate_line = jnp.broadcast_to(gate_line[None], (nd, 1, cols))
-    sent = jnp.concatenate([x_rows, dy_rows, gate_line], axis=1)
-    got = lax.all_to_all(sent, "dev", split_axis=0, concat_axis=0, tiled=True)
-    got = lax.all_gather(got, "node", axis=0, tiled=False)
+    gate_cols = jnp.broadcast_to(row_gate.astype(BF16)[None, :, None], (nd, rows, 128))
+    dy_rows = jnp.concatenate([dy_rows, gate_cols], axis=2)
+    x_got = lax.all_to_all(x_rows, "dev", split_axis=0, concat_axis=0, tiled=True)
+    x_got = lax.all_gather(x_got, "node", axis=0, tiled=False)
+    dy_got = lax.all_to_all(dy_rows, "dev", split_axis=0, concat_axis=0, tiled=True)
+    dy_got = lax.all_gather(dy_got, "node", axis=0, tiled=False)
     per_expert = nn * nd * PER
-    xs = got[:, :, :rows].reshape(nn, nd, experts, PER, cols).transpose(2, 0, 1, 3, 4)
+    xs = x_got.reshape(nn, nd, experts, PER, cols).transpose(2, 0, 1, 3, 4)
     xs = xs.reshape(experts, per_expert, cols)
-    dys = got[:, :, rows : 2 * rows].reshape(nn, nd, experts, PER, cols).transpose(2, 0, 1, 3, 4)
+    dys = dy_got[..., :cols].reshape(nn, nd, experts, PER, cols).transpose(2, 0, 1, 3, 4)
     dys = dys.reshape(experts, per_expert, cols)
-    gates = got[:, :, 2 * rows, :rows].reshape(nn, nd, experts, PER).transpose(2, 0, 1, 3)
+    gates = dy_got[..., cols].reshape(nn, nd, experts, PER).transpose(2, 0, 1, 3)
     part = experts * per_expert // nd
     gates = gates.reshape(nd, part)
     me = lax.axis_index("dev")
-    node = lax.axis_index("node")
     my_gate = jnp.sum(
         jnp.where(jnp.arange(nd)[:, None] == me, gates.astype(F32), 0.0), axis=0
     )[:, None]
@@ -65,36 +193,30 @@
         r = jnp.einsum(spec, a, b, preferred_element_type=F32).astype(BF16)
         return r.reshape(nd, part, hid)
 
-    pre = jnp.stack(
+    pre = jnp.concatenate(
         [
             widen(xs, w_gate, "jrd,jdh->jrh"),
             widen(xs, w_up, "jrd,jdh->jrh"),
             widen(dys, w_down, "jrd,jhd->jrh"),
         ],
-        axis=1,
-    )
-    pre = lax.all_to_all(pre, "dev", split_axis=0, concat_axis=0, tiled=True)
-    sums = jnp.sum(pre.astype(F32), axis=0)
-    gate_pre, up_pre, back = sums[0], sums[1], sums[2]
-    sig = jax.nn.sigmoid(gate_pre)
-    act = gate_pre * sig
-    hidden = act * up_pre
-    scaled = my_gate * back
-    d_gate = (scaled * up_pre * sig * (1.0 + gate_pre * (1.0 - sig))).astype(BF16)
-    d_up = (scaled * act).astype(BF16)
-    s_hid = (my_gate * hidden).astype(BF16)
-    gate_terms = jnp.sum(back * hidden, axis=-1)
-    full = lax.all_gather(jnp.stack([d_gate, d_up, s_hid]), "dev", axis=1, tiled=False)
-    full = full.reshape(3, experts, per_expert, hid)
-    spread = jnp.where(jnp.arange(nd)[:, None] == me, gate_terms[None, :], 0.0)
-    spread = lax.psum(spread.reshape(experts, nn, nd, PER), ("node", "dev"))
-    dg, du, sh = full[0], full[1], full[2]
+        axis=2,
+    )
+    full = middle(pre, jnp.broadcast_to(my_gate, (part, 128)), hid)
+    full = full.reshape(experts, per_expert, -1)
+    dg, du, sh = full[..., :hid], full[..., hid : 2 * hid], full[..., 2 * hid : 3 * hid]
+    terms = jnp.sum(full[..., 3 * hid :].astype(F32), axis=-1, keepdims=True)
     row_grad = jnp.einsum("jrh,jdh->jrd", dg, w_gate, preferred_element_type=F32)
     row_grad = row_grad + jnp.einsum("jrh,jdh->jrd", du, w_up, preferred_element_type=F32)
-    row_grad = row_grad.reshape(experts, nn, nd, PER, cols).transpose(1, 2, 0, 3, 4)
-    row_grad = lax.psum_scatter(row_grad, "node", scatter_dimension=0, tiled=False)
+    row_grad = jnp.concatenate(
+        [row_grad, jnp.broadcast_to(terms, terms.shape[:2] + (128,))], axis=2
+    )
+    row_grad = row_grad.reshape(experts, nn, nd, PER, cols + 128).transpose(1, 2, 0, 3, 4)
+    row_grad = row_grad.reshape(nn, nd, rows, cols + 128)
+    row_grad = lax.all_to_all(row_grad, "node", split_axis=0, concat_axis=0, tiled=True)
+    row_grad = jnp.sum(row_grad, axis=0)
     back_rows = lax.all_to_all(row_grad, "dev", split_axis=0, concat_axis=0, tiled=True)
-    back_rows = back_rows.reshape(nd, rows, cols).transpose(1, 0, 2).reshape(rows, width)
+    mine = back_rows[0, :, cols].reshape(experts, PER, 1)
+    back_rows = back_rows[:, :, :cols].transpose(1, 0, 2).reshape(rows, width)
     high = back_rows.astype(BF16)
     low = (back_rows - high.astype(F32)).astype(BF16)
     grad_tokens = jnp.einsum(
@@ -103,7 +225,6 @@
         jnp.concatenate([high, low], axis=0),
         preferred_element_type=F32,
     ).astype(BF16)
-    mine = lax.dynamic_slice(spread, (0, node, me, 0), (experts, 1, 1, PER)).reshape(experts, PER, 1)
     pair_val = jnp.sum(jnp.where(pick.reshape(experts, PER, tok) > 0, mine, 0.0), axis=1)
     grad_gates = jnp.sum(jnp.where(match, pair_val[:, :, None], 0.0), axis=0)
     grad_w_gate = jnp.einsum("jrd,jrh->jdh", xs, dg, preferred_element_type=F32).astype(BF16)

time: 243 us -> 202 us (0.83)
  waiting for transfers between devices: 102 us -> 13.4 us
  Pallas kernels: 0 us -> 52.5 us
  blocking collectives: 63.3 us -> 54.3 us
  starting transfers between devices: 10.3 us -> 13.5 us
    all_gather x2 -> x1, waiting for transfers between devices: 62.3 us -> 0.01 us  [local(): dy_got = lax.all_gather(dy_got, 'node', axis=0, tiled=False)]
    pallas_call x0 -> x1, Pallas kernels: none -> 52.5 us  [middle(): pl.pallas_call(functools.partial(middle_kernel, nd, hid), out_shape=jax.S...]
    psum x1 -> x0, blocking collectives: 39.9 us -> none  [local(): spread = lax.psum(spread.reshape(experts, nn, nd, PER), ('node', 'dev'))]
    all_to_all x1, waiting for transfers between devices: 36.2 us -> 8.08 us  [local(): lax.all_to_all(x_rows, 'dev', split_axis=0, concat_axis=0, tiled=True)]
    all_to_all x1 -> x2, blocking collectives: 23.4 us -> 45 us  [the longest x1 28.9 us: local(): lax.all_to_all(row_grad, 'node', split_axis=0, concat_axis=0, tiled=True)]
    all_gather x0 -> x1, blocking collectives: none -> 9.3 us  [local(): x_got = lax.all_gather(x_got, 'node', axis=0, tiled=False)]
    all_to_all x1, starting transfers between devices: 4.7 us -> 9.86 us  [local(): lax.all_to_all(row_grad, 'dev', split_axis=0, concat_axis=0, tiled=True)]
    dot_general x3, matrix products: 4.95 us -> 7.8 us  [widen(): r = jnp.einsum(spec, a, b, preferred_element_type=F32).astype(BF16)]
  transfers between devices with their start and end apart: 5 -> 3, of which waited for: 4 -> 2; matrix products, arithmetic and copies ran while one was open for 5% -> 9% of each run, Pallas kernels for 0% -> 0%
where the time goes in v2:
time: 202 us; the launch traced here: 201 us
  blocking collectives  54.3 us (27%)
  Pallas kernels  52.5 us (26%)
  matrix products  27.7 us (14%)
  local copies, waits for them, and re-layouts  16.2 us (8%)
  between operations  14.3 us (7%)
  starting transfers between devices  13.5 us (7%)
  waiting for transfers between devices  13.4 us (7%)
  other arithmetic  9 us (4%)
    pallas_call x1, Pallas kernels, middle(): pl.pallas_call(functools.partial(middle_kernel, nd, hid), out_shape=jax.S...  52.5 us
    all_to_all x1, blocking collectives, local(): lax.all_to_all(row_grad, 'node', split_axis=0, concat_axis=0, tiled=True)  28.9 us
    all_to_all x1, blocking collectives, local(): lax.all_to_all(dy_rows, 'dev', split_axis=0, concat_axis=0, tiled=True)  16.1 us
    all_to_all x1, starting transfers between devices, local(): lax.all_to_all(row_grad, 'dev', split_axis=0, concat_axis=0, tiled=True)  9.86 us
    all_gather x1, blocking collectives, local(): x_got = lax.all_gather(x_got, 'node', axis=0, tiled=False)  9.3 us
    all_to_all x1, waiting for transfers between devices, local(): lax.all_to_all(x_rows, 'dev', split_axis=0, concat_axis=0, tiled=True)  8.08 us
    dot_general x3, matrix products, widen(): r = jnp.einsum(spec, a, b, preferred_element_type=F32).astype(BF16)  7.8 us
    reshape x2, local copies, waits for them, and re-layouts, local(): row_grad.reshape(experts, nn, nd, PER, cols + 128).transpose(1, 2, 0, 3, 4)  6.07 us
  transfers between devices with their start and end apart: 3, of which 2 were waited for; matrix products, arithmetic and copies ran while one was open for 9% of the time, Pallas kernels for 0%

profile of v2, /device:TPU:0, one launch (start us, length us, event | category | flops | bytes accessed | tf_op | source)
XLA Modules:
  0.0 200.9 jit_solution(6580673773035371851)
XLA Ops:
  7.2 0.0 all-gather.4.cloned.1.call-start
  7.2 0.7 compare_reduce_fusion.1
  7.9 0.1 select_reduce_fusion
  8.0 0.1 select_reduce_fusion.4
  8.2 0.1 eq.71
  8.2 0.8 compare_reduce_fusion
  9.0 0.1 fusion.11
  9.2 0.7 convert_element_type.74
  9.9 0.8 fusion.13
  10.7 0.1 select_reduce_fusion.2
  10.8 0.1 convert_element_type.76
  10.9 0.1 compare_and_fusion
  11.0 2.6 %convolution_convert_fusion.1 = bf16[16,7168]{1,0:T(8,128)(2,1)S(1)} fusion(pred[16,256]{1,0:T(8,128)(4,1)S(1)} %compare_and_fusion, bf16[256,7168]{1,0:T(8,128)(2,1)} %param.9), kind=kOutput, calls=%fused_computation.1 | convolution fusion | flops 58834944 | bytes 3903488 | tf_op jit(solution)/shard_map/dot_general | solution.py:170
  13.6 0.1 broadcast_in_dim.122
  13.7 16.1 %all_to_all.20 = bf16[8,16,1024]{2,1,0:T(8,128)(2,1)} all-to-all(bf16[8,16,1024]{2,1,0:T(8,128)(2,1)S(1)} %pad_maximum_fusion.2), channel_id=1, replica_groups=mesh['node'=4,'dev'=8] {'dev'}, dimensions={0} | all-to-all | bytes 524288 | tf_op jit(solution)/shard_map/all_to_all | solution.py:177
  29.8 0.0 all-gather.4.cloned.1.call-update
  29.9 2.6 %convolution_convert_fusion.2 = bf16[16,7168]{1,0:T(8,128)(2,1)S(1)} fusion(pred[16,256]{1,0:T(8,128)(4,1)S(1)} %compare_and_fusion, bf16[256,7168]{1,0:T(8,128)(2,1)} %param.8), kind=kOutput, calls=%fused_computation.2 | convolution fusion | flops 58834944 | bytes 3903488 | tf_op jit(solution)/shard_map/dot_general | solution.py:169
  32.5 0.7 copy.123
  33.2 3.6 %all-to-all-start = ((bf16[8,16,896]{2,1,0:T(8,128)(2,1)}), bf16[8,16,896]{2,1,0:T(8,128)(2,1)S(1)}, u32[]{:S(2)}, u32[]{:S(2)}) async-start(bf16[8,16,896]{2,1,0:T(8,128)(2,1)} %bitcast.52), calls=%async_computation | async-start | bytes 458752 | tf_op jit(solution)/shard_map/all_to_all | solution.py:175
  36.8 8.1 %all-to-all-done = bf16[8,16,896]{2,1,0:T(8,128)(2,1)S(1)} async-done(((bf16[8,16,896]{2,1,0:T(8,128)(2,1)}), bf16[8,16,896]{2,1,0:T(8,128)(2,1)S(1)}, u32[]{:S(2)}, u32[]{:S(2)}) %all-to-all-start) | async-done | bytes 229408 | tf_op jit(solution)/shard_map/all_to_all | solution.py:175
  44.9 9.3 %all-gather = bf16[32,16,896]{2,1,0:T(8,128)(2,1)S(1)} all-gather(bf16[8,16,896]{2,1,0:T(8,128)(2,1)S(1)} %all-to-all-done), channel_id=2, replica_groups=mesh['node'=4,'dev'=8] {'node'}, dimensions={0}, use_global_device_ids=true | all-gather | bytes 1146880 | tf_op jit(solution)/shard_map/all_gather | solution.py:176
  54.2 0.2 reshape.95
  54.4 0.3 copy.121
  54.7 0.2 reshape.96
  54.9 0.0 copy-start
  55.0 2.9 %convolution_convert_fusion.7 = bf16[4,128,512]{2,1,0:T(8,128)(2,1)S(1)} fusion(bf16[4,128,896]{2,1,0:T(8,128)(2,1)S(1)} %reshape.96, bf16[4,896,512]{2,1,0:T(8,128)(2,1)} %param.14), kind=kOutput, calls=%fused_computation.10 | convolution fusion | flops 470024192 | bytes 5111808 | tf_op jit(solution)/shard_map/jrd,jdh->jrh/dot_general | solution.py:193
  57.9 0.2 copy-done
  58.1 1.5 convolution_convert_fusion.8
  59.6 0.9 slice.37
  60.6 1.3 slice.36
  61.8 0.2 copy.114
  62.1 0.2 copy.100
  62.3 0.4 copy.101
  62.7 0.2 reshape.101
  62.9 0.1 copy.103
  63.0 0.2 copy.104
  63.1 0.1 reshape.107
  63.2 0.1 select_reduce_fusion.3
  63.3 3.3 %convolution_convert_fusion.6 = bf16[4,128,512]{2,1,0:T(8,128)(2,1)S(1)} fusion(bf16[4,128,896]{2,1,0:T(8,128)(2,1)S(1)} %reshape.101, bf16[4,512,896]{2,1,0:T(8,128)(2,1)} %param.15), kind=kOutput, calls=%fused_computation.9 | convolution fusion | flops 470024192 | bytes 5111808 | tf_op jit(solution)/shard_map/jrd,jhd->jrh/dot_general | solution.py:193
  66.7 0.1 pad_maximum_fusion.1.pre
  66.8 0.1 broadcast_in_dim.125.gate
  66.9 52.5 %shard_map.119 = bf16[8,64,1664]{2,1,0:T(8,128)(2,1)S(1)} custom-call(bf16[8,64,1536]{2,1,0:T(8,128)(2,1)S(1)} %pad_maximum_fusion.1.pre, f32[64,128]{1,0:T(8,128)S(1)} %broadcast_in_dim.125.gate), custom_call_target="tpu_custom_call" | custom-call | tf_op jit(solution)/shard_map/pallas_call | solution.py:117
  119.5 0.4 fusion.9
  119.8 0.0 copy-done.1
  119.8 1.3 fusion.4
  121.1 0.4 copy-done.2
  121.5 1.3 convolution_add_fusion
  122.8 1.6 pad_maximum_fusion
  124.3 2.8 %reshape.104 = f32[4,4,8,4,1024]{4,3,2,1,0:T(4,128)} reshape(f32[4,128,1024]{2,1,0:T(8,128)} %pad_maximum_fusion) | data formatting | bytes 4194304 | tf_op jit(solution)/shard_map/reshape | solution.py:213
  127.2 3.2 %copy.105 = f32[4,4,8,4,1024]{4,2,3,0,1:T(8,128)S(1)} copy(f32[4,4,8,4,1024]{4,3,2,1,0:T(4,128)} %reshape.104) | data formatting | bytes 4194304 | tf_op jit(solution)/shard_map/reshape | solution.py:213
  130.4 28.9 %all_to_all.21 = f32[4,8,16,1024]{3,1,2,0:T(8,128)} all-to-all(f32[4,8,16,1024]{3,1,2,0:T(8,128)S(1)} %bitcast.59), channel_id=1, replica_groups=mesh['node'=4,'dev'=8] {'node'}, dimensions={0} | all-to-all | bytes 4194304 | tf_op jit(solution)/shard_map/all_to_all | solution.py:215
  159.3 2.6 %reduce_sum.87 = f32[8,16,1024]{2,0,1:T(8,128)} reduce(f32[4,8,16,1024]{3,1,2,0:T(8,128)} %all_to_all.21, f32[]{:T(128)} %constant.4.clone.1), dimensions={0}, to_apply=%region_7.8 | reduce | flops 393216 | bytes 2621444 | tf_op jit(solution)/shard_map/reduce_sum | solution.py:216
  161.9 2.1 %copy.106 = f32[8,16,1024]{2,1,0:T(8,128)} copy(f32[8,16,1024]{2,0,1:T(8,128)} %reduce_sum.87) | data formatting | bytes 1048576 | tf_op jit(solution)/shard_map/reduce_sum | solution.py:216
  164.1 9.9 %all-to-all-start.3 = ((f32[8,16,1024]{2,1,0:T(8,128)}), f32[8,16,1024]{2,1,0:T(8,128)}, u32[]{:S(2)}, u32[]{:S(2)}) async-start(f32[8,16,1024]{2,1,0:T(8,128)} %copy.106), calls=%async_computation.3 | async-start | bytes 1048576 | tf_op jit(solution)/shard_map/all_to_all | solution.py:217
  173.9 3.0 %convolution_convert_fusion.3 = bf16[4,512,896]{2,1,0:T(8,128)(2,1)} fusion(bf16[4,128,896]{2,1,0:T(8,128)(2,1)S(1)} %reshape.101, bf16[4,128,1664]{2,1,0:T(8,128)(2,1)S(1)} %bitcast.56), kind=kOutput, calls=%fused_computation.3 | convolution fusion | flops 471597056 | bytes 5111808 | tf_op jit(solution)/shard_map/jrh,jrd->jhd/dot_general | solution.py:232
  176.9 3.0 %convolution_convert_fusion.5 = bf16[4,896,512]{2,1,0:T(8,128)(2,1)} fusion(bf16[4,128,896]{2,1,0:T(8,128)(2,1)S(1)} %reshape.96, bf16[4,128,1664]{2,1,0:T(8,128)(2,1)S(1)} %bitcast.57), kind=kOutput, calls=%fused_computation.5 | convolution fusion | flops 471597056 | bytes 5111808 | tf_op jit(solution)/shard_map/jrd,jrh->jdh/dot_general | solution.py:230
  179.9 3.0 %convolution_convert_fusion.4 = bf16[4,896,512]{2,1,0:T(8,128)(2,1)} fusion(bf16[4,128,896]{2,1,0:T(8,128)(2,1)S(1)} %reshape.96, bf16[4,128,1664]{2,1,0:T(8,128)(2,1)S(1)} %bitcast.58), kind=kOutput, calls=%fused_computation.4 | convolution fusion | flops 471597056 | bytes 5111808 | tf_op jit(solution)/shard_map/jrd,jrh->jdh/dot_general | solution.py:231
  182.9 5.3 %all-to-all-done.3 = f32[8,16,1024]{2,1,0:T(8,128)} async-done(((f32[8,16,1024]{2,1,0:T(8,128)}), f32[8,16,1024]{2,1,0:T(8,128)}, u32[]{:S(2)}, u32[]{:S(2)}) %all-to-all-start.3) | async-done | bytes 524320 | tf_op jit(solution)/shard_map/all_to_all | solution.py:217
  188.2 1.0 slice_bitcast_fusion
  189.3 0.8 slice_reduce_fusion
  190.2 0.1 broadcast_in_dim.127
  190.2 0.1 select_reduce_fusion.1
  190.4 0.7 fusion.14
  191.0 3.0 %convolution_convert_fusion = bf16[256,7168]{1,0:T(8,128)(2,1)} fusion(bf16[16,7168]{1,0:T(8,128)(2,1)S(1)} %get-tuple-element.5, bf16[16,7168]{1,0:T(8,128)(2,1)S(1)} %get-tuple-element.6, pred[16,256]{1,0:T(8,128)(4,1)S(1)} %compare_and_fusion), kind=kOutput, calls=%fused_computation | convolution fusion | flops 120201216 | bytes 4132864 | tf_op jit(solution)/shard_map/qt,qd->td/dot_general | solution.py:222
  (17 shorter events, 0.2 us)
Async XLA Ops:
  7.2 52.5 %all-gather.4.cloned.1.call-start = ((), (), s32[]{:S(2)}) async-start(), calls=%async_computation.4 | async-start | bytes 1310720 | tf_op jit(solution)/shard_map/all_gather | solution.py:178
  33.2 11.7 %all-to-all-start = ((bf16[8,16,896]{2,1,0:T(8,128)(2,1)}), bf16[8,16,896]{2,1,0:T(8,128)(2,1)S(1)}, u32[]{:S(2)}, u32[]{:S(2)}) async-start(bf16[8,16,896]{2,1,0:T(8,128)(2,1)} %bitcast.52), calls=%async_computation | async-start | bytes 458752 | tf_op jit(solution)/shard_map/all_to_all | solution.py:175
  54.9 3.1 %copy-start = (bf16[4,896,512]{2,1,0:T(8,128)(2,1)S(1)}, bf16[4,896,512]{2,1,0:T(8,128)(2,1)}, u32[]{:S(2)}) copy-start(bf16[4,896,512]{2,1,0:T(8,128)(2,1)} %param.13) | copy-start | bytes 11010052
  62.9 3.8 %copy-start.3 = (bf16[4,128,512]{2,1,0:T(8,128)(2,1)S(1)}, bf16[4,128,512]{2,1,0:T(8,128)(2,1)}, u32[]{:S(2)}) copy-start(bf16[4,128,512]{2,1,0:T(8,128)(2,1)} %convolution_convert_fusion.8) | copy-start | bytes 1572868
  66.7 53.2 %copy-start.1 = (bf16[4,896,512]{2,1,0:T(8,128)(2,1)S(1)}, bf16[4,896,512]{2,1,0:T(8,128)(2,1)}, u32[]{:S(2)}) copy-start(bf16[4,896,512]{2,1,0:T(8,128)(2,1)} %param.13) | copy-start | bytes 11010052
  119.4 2.0 %copy-start.2 = (bf16[4,896,512]{2,1,0:T(8,128)(2,1)S(1)}, bf16[4,896,512]{2,1,0:T(8,128)(2,1)}, u32[]{:S(2)}) copy-start(bf16[4,896,512]{2,1,0:T(8,128)(2,1)} %param.14) | copy-start | bytes 11010052
  164.1 24.1 %all-to-all-start.3 = ((f32[8,16,1024]{2,1,0:T(8,128)}), f32[8,16,1024]{2,1,0:T(8,128)}, u32[]{:S(2)}, u32[]{:S(2)}) async-start(f32[8,16,1024]{2,1,0:T(8,128)} %copy.106), calls=%async_computation.3 | async-start | bytes 1048576 | tf_op jit(solution)/shard_map/all_to_all | solution.py:217
  179.9 10.4 %copy-start.4 = (s32[256,8]{0,1:T(8,128)S(1)}, s32[256,8]{0,1:T(8,128)}, u32[]{:S(2)}) copy-start(s32[256,8]{0,1:T(8,128)} %param.11) | copy-start | bytes 24580
Sparse Core Ops, SparseCore 0:
  30.0 15.7 all-gather.3
